TPU v7x, 32 devices: a whole 2x2x4 slice. The times are simulated.
32 devices in a mesh: dp: 16 (over z, y, core), mp: 2 (over x).
Axes of the slice: x: 2, y: 2, z: 4, core: 2. Of those that a mesh axis runs over, the one named last changes fastest.
Arguments:
- tokens: bfloat16 [23040, 768], P('dp'), may hold values from -6 to 6
- cotangent: bfloat16 [23040, 768], P('dp'), may hold values from -6 to 6
- lengths: int32 [80], P('dp'), may hold values from 72 to 288, as said below
- doc_ids: int32 [80, 8], P('dp'), may hold values from 0 to 127
- doc_rows: bfloat16 [80, 8, 128], P('dp'), may hold values from -6 to 6
- w_qkv: float32 [3, 768, 768], P(None, 'dp', 'mp'), may hold values from -0.21875 to 0.21875
- m_qkv: float32 [3, 768, 768], P(None, 'dp', 'mp'), may hold values from -0.00061035156 to 0.00061035156
- v_qkv: float32 [3, 768, 768], P(None, 'dp', 'mp'), may hold values from 6.958547e-11 to 1.1133675e-09
- w_attn: float32 [768, 768], P('dp', 'mp'), may hold values from -0.875 to 0.875
- m_attn: float32 [768, 768], P('dp', 'mp'), may hold values from -0.00061035156 to 0.00061035156
- v_attn: float32 [768, 768], P('dp', 'mp'), may hold values from 6.958547e-11 to 1.1133675e-09
- w_inner: float32 [768, 3072], P('dp', 'mp'), may hold values from -0.21875 to 0.21875
- m_inner: float32 [768, 3072], P('dp', 'mp'), may hold values from -0.00061035156 to 0.00061035156
- v_inner: float32 [768, 3072], P('dp', 'mp'), may hold values from 6.958547e-11 to 1.1133675e-09
- w_outer: float32 [768, 3072], P('dp', 'mp'), may hold values from -0.109375 to 0.109375
- m_outer: float32 [768, 3072], P('dp', 'mp'), may hold values from -0.00061035156 to 0.00061035156
- v_outer: float32 [768, 3072], P('dp', 'mp'), may hold values from 6.958547e-11 to 1.1133675e-09
- w_proj: float32 [768, 128], P('dp'), may hold values from -0.21875 to 0.21875
- m_proj: float32 [768, 128], P('dp'), may hold values from -3.0517578e-05 to 3.0517578e-05
- v_proj: float32 [768, 128], P('dp'), may hold values from 1.9329297e-13 to 2.8993947e-12
- vectors: float32 [12, 768], P(None, ('dp', 'mp')), may hold values from -1.2 to 2.5, as said below
- m_vectors: float32 [12, 768], P(None, ('dp', 'mp')), may hold values from -0.005859375 to 0.005859375
- v_vectors: float32 [12, 768], P(None, ('dp', 'mp')), may hold values from 6.958547e-09 to 1.1133675e-07
Outputs:
- out_tokens: bfloat16 [23040, 768], P('dp')
- input_grad: float32 [23040, 768], P('dp')
- grad_norm: float32 [], replicated
- qkv_first: float32 [3, 768, 768], P(None, 'dp', 'mp')
- qkv_second: float32 [3, 768, 768], P(None, 'dp', 'mp')
- qkv_new: float32 [3, 768, 768], P(None, 'dp', 'mp')
- attn_first: float32 [768, 768], P('dp', 'mp')
- attn_second: float32 [768, 768], P('dp', 'mp')
- attn_new: float32 [768, 768], P('dp', 'mp')
- inner_first: float32 [768, 3072], P('dp', 'mp')
- inner_second: float32 [768, 3072], P('dp', 'mp')
- inner_new: float32 [768, 3072], P('dp', 'mp')
- outer_first: float32 [768, 3072], P('dp', 'mp')
- outer_second: float32 [768, 3072], P('dp', 'mp')
- outer_new: float32 [768, 3072], P('dp', 'mp')
- proj_first: float32 [768, 128], P('dp')
- proj_second: float32 [768, 128], P('dp')
- proj_new: float32 [768, 128], P('dp')
- vector_first: float32 [12, 768], P(None, ('dp', 'mp'))
- vector_second: float32 [12, 768], P(None, ('dp', 'mp'))
- vector_new: float32 [12, 768], P(None, ('dp', 'mp'))
- table_grad: float32 [128, 128], P('dp')
Inputs may be any that keep to these rules, and one draw needn't show every extreme that they name: `lengths`: real tokens of each sequence; positions past it are padding keys; some sequence has all 288. `vectors`: norm gains positive, other rows of either sign.
All inputs are finite; a program needn't handle non-finite values.
Results may differ from a plain program's by a relative error of at most 0.012.
The roundings to bfloat16 on the way count: a program that leaves them out, or rounds other values in their place, can miss the bound.
Values may be sent and summed in bfloat16 or wider, within the bound.
A program may use at most 192 MiB of HBM per device.

v0:
```python
import functools

import jax
import jax.numpy as jnp
from jax import lax
from jax.experimental import pallas as pl
from jax.experimental.pallas import tpu as pltpu
from jax.sharding import PartitionSpec as P

HEAD_DIM = 64
STEP = 10
TAB_DEV = 8
MESH = pl.DeviceIdType.MESH
ANY = pl.ANY
BF = jnp.bfloat16
F32 = jnp.float32
NZ, NY, NC, NX = 4, 2, 2, 2

highest_mode = lax.Precision.HIGHEST
retrieval_scale = 0.17677669529663687
ln_epsilon = 1e-12
beta_first = 0.9
beta_second = 0.999
learn_rate = 0.05
vector_rate = 0.5
decay_rate = 0.01
adam_epsilon = 1e-08
clip_norm = 1.0


def layer_norm(values, gain_row, shift_row):
    centre = jnp.mean(values, axis=-1, keepdims=True)
    centred = values - centre
    spread = jnp.mean(centred * centred, axis=-1, keepdims=True)
    return centred * lax.rsqrt(spread + ln_epsilon) * gain_row + shift_row


def gelu_exact(values):
    return jax.nn.gelu(values, approximate=False)


def adamw_update(weight, moment, second, gradient, decay_factor, step_rate):
    moment_new = beta_first * moment + (1.0 - beta_first) * gradient
    second_new = beta_second * second + (1.0 - beta_second) * gradient * gradient
    first_hat = moment_new / (1.0 - beta_first**STEP)
    second_hat = second_new / (1.0 - beta_second**STEP)
    weight_new = weight - step_rate * (
        first_hat / (jnp.sqrt(second_hat) + adam_epsilon) + decay_factor * weight
    )
    return (moment_new, second_new, weight_new)


def squared(values):
    return jnp.sum(values * values)


class Place:
    def __init__(self):
        dp = lax.axis_index("dp")
        self.x = lax.axis_index("mp")
        self.c = lax.rem(dp, NC)
        self.y = lax.rem(dp // NC, NY)
        self.z = dp // (NC * NY)

    def dev(self, z=None, y=None, c=None, x=None):
        z = self.z if z is None else z
        y = self.y if y is None else y
        c = self.c if c is None else c
        x = self.x if x is None else x
        return ((z * NY + y) * NC + c, x)

    def others(self):
        out = [self.dev(z=lax.rem(self.z + k, NZ)) for k in range(1, NZ)]
        out.append(self.dev(x=1 - self.x))
        out.append(self.dev(y=1 - self.y))
        out.append(self.dev(c=1 - self.c))
        return out

    def eights(self):
        out = []
        for k in range(1, 8):
            dx, dy, dc = k & 1, (k >> 1) & 1, k >> 2
            out.append(
                self.dev(
                    x=self.x + dx - 2 * dx * self.x,
                    y=self.y + dy - 2 * dy * self.y,
                    c=self.c + dc - 2 * dc * self.c,
                )
            )
        return out


def greet(devices):
    barrier = pltpu.get_barrier_semaphore()
    for d in devices:
        pl.semaphore_signal(barrier, inc=1, device_id=d, device_id_type=MESH)
    pl.semaphore_wait(barrier, len(devices))


def greet_send(devices):
    barrier = pltpu.get_barrier_semaphore()
    for d in devices:
        pl.semaphore_signal(barrier, inc=1, device_id=d, device_id_type=MESH)


def greet_wait(count):
    pl.semaphore_wait(pltpu.get_barrier_semaphore(), count)


def remote(src, dst, ssem, rsem, dev):
    return pltpu.make_async_remote_copy(
        src_ref=src, dst_ref=dst, send_sem=ssem, recv_sem=rsem, device_id=dev, device_id_type=MESH
    )


def cols(x, half):
    return pl.ds(pl.multiple_of(x * half, 128), half)


def dma(*shape):
    return pltpu.SemaphoreType.DMA(shape)


def mm(a, b):
    return jnp.dot(a, b, preferred_element_type=F32)


def mm_nt(a, b):
    return lax.dot_general(a, b, (((1,), (1,)), ((), ())), preferred_element_type=F32)


def mm_tn(a, b):
    return lax.dot_general(a, b, (((0,), (0,)), ((), ())), preferred_element_type=F32)


def flat(value):
    return value.reshape(-1, value.shape[-1])


def lanes(i, n=128):
    return pl.ds(pl.multiple_of(i * n, 128), n)


def rows_at(i, n, at=0):
    return pl.ds(pl.multiple_of(at + i * n, 16), n)


def each(n, body):
    lax.fori_loop(0, n, lambda i, c: (body(i), c)[1], 0)


gather_orders = ("zxy", "zxy", "yzx", "zxy", "zyx", "zxy", "zyx", "zxy", "zyx", "zxy", "zyx", "zxy", "xyz", "yxz", "zyx")


def with_jobs(n, body, go, jobs):
    def one(i):
        body(i)
        for at, todo in enumerate(jobs):
            if todo:

                @pl.when(i == at)
                def _(todo=todo):
                    for job in todo:
                        go(*job)

    each(n, one)


def stack_heads(pair, wide=None):
    low = jnp.where(lax.broadcasted_iota(jnp.int32, (1, 128), 1) < HEAD_DIM, 1.0, 0.0)
    parts = []
    for mask in (low, 1.0 - low):
        parts.append(pair * mask.astype(BF))
        if wide is not None:
            parts.append(jnp.zeros((wide - pair.shape[0], 128), BF))
    return jnp.concatenate(parts, axis=0)


class Gather:
    def __init__(self, me, pieces, sems):
        self.me, self.pieces = me, pieces
        self.lsem, self.ss, self.rs, self.ds, self.dr = sems
        self.waits = []

    def region(self, p, stage, c, **at):
        dst, me, done = self.pieces[p][1], self.me, gather_orders[p][:stage]
        half = dst.shape[-1] // 2
        z = at.get("z", None if "z" in done else me.z)
        y = at.get("y", None if "y" in done else me.y)
        x = at.get("x", None if "x" in done else me.x)
        zs = slice(None) if z is None else pl.ds(0, NZ - 1) if z == "three" else pl.ds(z, 1)
        ys = slice(None) if y is None else pl.ds(y, 1)
        xs = slice(None) if x is None else cols(x, half)
        return dst.at[zs, ys, c, :, xs]

    def bulk(self, p, stage, c):
        axis = gather_orders[p][stage]
        return self.region(p, stage, c, z="three") if axis == "z" else self.coming(p, stage, c)[0]

    def coming(self, p, stage, c):
        me, axis = self.me, gather_orders[p][stage]
        if axis == "z":
            return [self.region(p, stage, c, z=lax.rem(me.z + NZ - k, NZ)) for k in range(1, NZ)]
        return [self.region(p, stage, c, **{axis: 1 - (me.y if axis == "y" else me.x)})]

    def send(self, p, stage):
        me, axis = self.me, gather_orders[p][stage]
        src, dst = self.pieces[p]
        if stage == 0:
            to = dst.at[me.z, me.y, me.c, :, cols(me.x, dst.shape[-1] // 2)]
        else:
            src = to = self.region(p, stage, me.c)
        if axis == "z":
            devs = [me.dev(z=lax.rem(me.z + k, NZ)) for k in range(1, NZ)]
        else:
            devs = [me.dev(**{axis: 1 - (me.y if axis == "y" else me.x)})]
        for dev in devs:
            remote(src, to, self.ss.at[p, stage], self.rs.at[p, stage], dev).start()
        self.waits.append((p, stage, False))

    def arrived(self, ref, sem):
        remote(ref, ref, sem, sem, self.me.dev(c=1 - self.me.c)).wait_recv()

    def receive(self, p, stage):
        self.arrived(self.bulk(p, stage, self.me.c), self.rs.at[p, stage])

    def crossing(self, p, stage, c):
        if stage == 0:
            ref = self.region(p, 1, c)
            return [ref], ref
        return self.coming(p, stage, c), self.bulk(p, stage, c)

    def cross(self, p, stage):
        refs = self.crossing(p, stage, self.me.c)[0]
        for ref in refs:
            remote(ref, ref, self.ds.at[p, stage], self.dr.at[p, stage], self.me.dev(c=1 - self.me.c)).start()
        self.waits.append((p, stage, True))

    def own_copy(self, p):
        me = self.me
        src, dst = self.pieces[p]
        blk = dst.at[me.z, me.y, me.c, :, cols(me.x, dst.shape[-1] // 2)]
        return pltpu.make_async_copy(src, blk, self.lsem.at[p])

    def step1(self, p):
        self.send(p, 0)
        self.own_copy(p).start()

    def step2(self, p):
        self.own_copy(p).wait()
        self.receive(p, 0)
        self.send(p, 1)
        self.cross(p, 0)

    def step3(self, p):
        self.receive(p, 1)
        self.send(p, 2)
        self.cross(p, 1)

    def step4(self, p):
        self.receive(p, 2)
        self.cross(p, 2)

    def step5(self, p):
        for stage in range(3):
            self.arrived(self.crossing(p, stage, 1 - self.me.c)[1], self.dr.at[p, stage])

    def end(self):
        c = self.me.c
        for p, stage, over in self.waits:
            ref = self.crossing(p, stage, c)[1] if over else self.bulk(p, stage, c)
            sem = (self.ds if over else self.ss).at[p, stage]
            remote(ref, ref, sem, sem, self.me.dev(c=1 - c)).wait_send()


def norm_rows(z_ref, r_ref, n_rows, put):
    step = 48

    def body(i):
        at = rows_at(i, step)
        z = z_ref[at, :]
        centred = z - jnp.mean(z, axis=-1, keepdims=True)
        spread = jnp.mean(centred * centred, axis=-1, keepdims=True)
        root = lax.rsqrt(spread + ln_epsilon)
        hat = centred * root
        z_ref[at, :] = hat
        r_ref[at, :] = jnp.broadcast_to(root, (step, 128))
        put(at, hat)

    each(n_rows // step, body)


def forward_kernel(*refs):
    (lens, tokens, w_qkv, w_attn, w_inner, w_outer, w_proj, vectors) = refs[:8]
    outs = refs[8:27]
    scr = refs[27:]
    (vec_s, proj_s, qk_s, va_s, inner_s, outer_s, vec_g, proj_g, qk, va, inner, outer) = scr[:12]
    (xt, q, k, v, p, o, xh1, r1, g, gp, xh2, r2, out_own, proj, vec, x_all, h1b, vecp, bias_ff) = scr[12:31]
    gsems, tsem, osem = scr[31:36], scr[36], scr[37]
    me = Place()
    mp = me.x
    n_all, width = x_all.shape
    n_own = q.shape[0]
    half_seq = n_all - n_own
    seq = 2 * half_seq
    full = (n_own - half_seq) // seq
    n_full = full * seq
    half_ff = inner.shape[-1]
    rows = qk_s.shape[1]
    half_rows = rows // 2

    starts = (
        (mp * (n_full + seq), 0, n_full),
        (n_full + mp * half_seq, n_full, half_seq),
        (n_full + (1 - mp) * half_seq, n_own, half_seq),
    )
    loads = []
    for i, (at, to, n) in enumerate(starts):
        cp = pltpu.make_async_copy(
            tokens.at[pl.ds(pl.multiple_of(at, 16), n)], x_all.at[pl.ds(to, n)], tsem.at[i]
        )
        cp.start()
        loads.append(cp)

    greet_send(me.others())
    vecp[...] = jnp.zeros_like(vecp)
    nvec, nlane = vectors.shape
    vecp[0:nvec, 0:nlane] = vectors[...]
    proj_s[...] = w_proj[pl.ds(pl.multiple_of(mp * half_rows, 8), half_rows), :]
    vec_s[...] = jnp.transpose(vecp[...])[0:nlane]
    qk_s[...] = w_qkv[0:2].astype(BF)
    va_s[0] = w_qkv[2].astype(BF)
    va_s[1] = w_attn[...].astype(BF)
    hf = half_ff // 2
    for h in range(2):
        inner_s[h] = w_inner[:, h * hf : (h + 1) * hf].astype(BF)
        outer_s[h] = w_outer[:, h * hf : (h + 1) * hf].astype(BF)

    greet_wait(len(me.others()))
    row_cut = 32
    pieces = [
        (vec_s, vec_g),
        (qk_s.at[0], qk.at[0]),
        (qk_s.at[1], qk.at[1]),
        (va_s.at[0, pl.ds(0, row_cut)], va.at[0, :, :, :, pl.ds(0, row_cut)]),
        (va_s.at[0, pl.ds(row_cut, rows - row_cut)], va.at[0, :, :, :, pl.ds(row_cut, rows - row_cut)]),
        (va_s.at[1], va.at[1]),
    ]
    for shard, whole in ((inner_s, inner), (outer_s, outer)):
        for h in range(2):
            for j in range(2):
                src = shard.at[h, :, pl.ds(j * (hf // 2), hf // 2)]
                pieces.append((src, whole.at[h, :, :, :, :, pl.ds(j * hf, hf)]))
    pieces.append((proj_s, proj_g))
    net = Gather(me, pieces, gsems)

    def go(step, *members):
        for piece in members:
            (net.step1, net.step2, net.step3, net.step4, net.step5)[step - 1](piece)

    go(1, 0, 1, 2, 12, 13)
    saves = []

    def save(i, ref):
        cp = pltpu.make_async_copy(ref, outs[i], osem.at[i])
        cp.start()
        saves.append(cp)

    for cp in loads:
        cp.wait()

    def x_turn(i):
        xt[rows_at(i, 256), :] = jnp.transpose(x_all[:, lanes(i, 256)])

    each(width // 256, x_turn)
    save(4, xt)
    go(2, 2, 0)
    go(1, 3, 4)
    go(2, 1, 12, 13)
    go(1, 5)
    go(3, 0, 1, 2)
    go(1, 6)
    go(2, 3, 4)
    go(1, 7)
    go(4, 0)
    go(5, 0)
    big = []
    for z in range(NZ):
        for y in range(NY):
            for c in range(NC):
                for x in range(NX):
                    big.append(vec_g[z, y, c, :, x * 128 : (x + 1) * 128])
    vec[...] = jnp.transpose(jnp.concatenate(big, axis=0))[0 : vec.shape[0]]
    for h in range(2):
        for x in range(NX):
            for j in range(2):
                row = vec[5 + NX * x + h : 6 + NX * x + h, j * (hf // 2) : (j + 1) * (hf // 2)]
                bias_ff[h : h + 1, j * hf + x * (hf // 2) : j * hf + (x + 1) * (hf // 2)] = row
    save(17, vec)

    def project(w_ref, src_rows, dst, bias):
        n_tile = 256

        def body(i):
            w = flat(w_ref[:, :, :, :, lanes(i, n_tile)])
            r = mm(x_all[0:src_rows], w)
            if bias is not None:
                r = r + vec[bias : bias + 1, lanes(i, n_tile)]
            dst[:, lanes(i, n_tile)] = r.astype(BF)

        each(width // n_tile, body)

    go(3, 3)
    go(4, 1)
    go(3, 4)
    go(2, 5)
    go(1, 8)
    go(4, 2)
    go(5, 1)
    project(qk.at[0], n_own, q, 0)
    go(5, 2)
    go(2, 6)
    go(1, 9)
    project(qk.at[1], n_all, k, None)
    save(0, qk)
    go(4, 3, 4)
    go(3, 5)
    go(5, 3, 4)
    project(va.at[0], n_all, v, 1)
    go(2, 7)
    go(3, 6)
    go(1, 10)
    save(5, q)
    save(6, k)
    save(7, v)

    wide = 384
    pos = lax.broadcasted_iota(jnp.int32, (1, wide), 1)
    beyond = jnp.where(pos < seq, 0, 1 << 20)

    def attend(q0, nq, k0, slab, length, place):
        at_q = pl.ds(pl.multiple_of(q0, 16), nq)
        at_k = pl.ds(pl.multiple_of(k0, 16), seq)
        for pair in range(2):
            l = lanes(2 * slab + pair)
            s = mm_nt(q[at_q, l], stack_heads(k[at_k, l], wide)) * (HEAD_DIM**-0.5)
            both = []
            for h in range(2):
                part = jnp.where(place < length, s[:, h * wide : (h + 1) * wide], -1000000000.0)
                e = jnp.exp(part - jnp.max(part, axis=-1, keepdims=True))
                both.append((e * (1.0 / jnp.sum(e, axis=-1, keepdims=True))).astype(BF))
            pb = jnp.concatenate(both, axis=1)
            p[slab, at_q, 2 * wide * pair : 2 * wide * (pair + 1)] = pb
            o[at_q, l] = mm(pb, stack_heads(v[at_k, l], wide)).astype(BF)

    slabs = p.shape[0]
    jobs = [[(2, 8), (1, 11, 14), (3, 12)], [(3, 7)], [(2, 9)], [(4, 5), (3, 13)], [(2, 10), (4, 6)], [(3, 8), (5, 5, 6)]]
    for s in range(full):
        length = lens[mp * (full + 1) + s]
        with_jobs(slabs, lambda i: attend(s * seq, seq, s * seq, i, length, pos + beyond), go, jobs[3 * s : 3 * s + 3])
    length = lens[full]
    pos_c = jnp.where(pos < half_seq, pos + mp * half_seq, pos - half_seq + (1 - mp) * half_seq) + beyond
    with_jobs(slabs, lambda i: attend(n_full, half_seq, n_full, i, length, pos_c), go, [[], [(3, 9)], []])
    go(2, 11, 14)
    save(8, p)
    save(9, o)

    tile = 720
    tiles = n_own // tile

    def attn_out(i):
        a = mm_nt(o[rows_at(i, tile), :], flat(va[1]))
        xh1[rows_at(i, tile), :] = x_all[rows_at(i, tile), :].astype(F32) + a + vec[2:3, :]

    each(tiles, attn_out)
    go(4, 7)
    save(1, va)

    def put_h1(at, hat):
        h1b[at, :] = (hat * vec[3:4, :] + vec[4:5, :]).astype(BF)

    norm_rows(xh1, r1, n_own, put_h1)
    save(10, xh1)
    save(11, r1)
    go(5, 7)
    go(3, 10)
    go(4, 8)

    def feed(h):
        n_tile = 256

        def body(i):
            w = flat(inner[h, :, :, :, :, lanes(i, n_tile)])
            for t in range(tiles):
                at = pl.ds(t * tile, tile)
                u = mm(h1b[at, :], w)
                u = u + bias_ff[h : h + 1, lanes(i, n_tile)]
                tail = 0.5 * (1.0 + lax.erf(u * 0.7071067811865476))
                g[h, at, lanes(i, n_tile)] = (u * tail).astype(BF)
                slope = tail + u * (0.3989422804014327 * jnp.exp(-0.5 * u * u))
                gp[h, at, lanes(i, n_tile)] = slope.astype(BF)

        each(half_ff // n_tile, body)

    feed(0)
    go(3, 11)
    go(5, 8)
    go(4, 9)
    go(5, 9)
    feed(1)
    go(3, 14)
    go(4, 10, 12, 11, 13)
    go(5, 10, 12, 11, 13)
    save(2, inner)
    save(12, g)
    save(13, gp)

    def ff_out(i):
        at = rows_at(i, tile)
        f = mm_nt(g[0, at, :], flat(outer[0])) + mm_nt(g[1, at, :], flat(outer[1]))
        h1 = xh1[at, :] * vec[3:4, :] + vec[4:5, :]
        xh2[at, :] = h1 + f + vec[9:10, :]

    each(tiles, ff_out)
    save(3, outer)
    go(4, 14)

    def put_y(at, hat):
        out_own[at, :] = (hat * vec[10:11, :] + vec[11:12, :]).astype(BF)

    norm_rows(xh2, r2, n_own, put_y)
    save(14, xh2)
    save(15, r2)
    save(18, out_own)
    go(5, 14)
    for d in range(NZ * NY * NC * NX):
        block = proj_g[d // 8, d // 4 % 2, d // 2 % 2, :, d % 2 * 128 : (d % 2 + 1) * 128]
        proj[d * half_rows : (d + 1) * half_rows] = block
    save(16, proj)
    net.end()
    for cp in saves:
        cp.wait()


def forward_fast(lengths, tokens, w_qkv, w_attn, w_inner, w_outer, w_proj, vectors):
    seqs = lengths.shape[0]
    all_rows, width = tokens.shape
    seq = all_rows // seqs
    full = seqs // 2
    n_own = full * seq + seq // 2
    n_all = n_own + seq // 2
    rows, half_ff = w_qkv.shape[1], w_inner.shape[1]
    heads = width // HEAD_DIM
    zyc = (NZ, NY, NC)
    hr, nlane = rows // 2, vectors.shape[1]
    weights = [
        ((2,) + zyc + (rows, width), BF),
        ((2,) + zyc + (rows, width), BF),
        ((2,) + zyc + (rows, half_ff), BF),
        ((2,) + zyc + (rows, half_ff), BF),
    ]
    kept = [
        ((width, n_all), BF),
        ((n_own, width), BF),
        ((n_all, width), BF),
        ((n_all, width), BF),
        ((heads // 4, n_own, 4 * 384), BF),
        ((n_own, width), BF),
        ((n_own, width), F32),
        ((n_own, 128), F32),
        ((2, n_own, half_ff), BF),
        ((2, n_own, half_ff), BF),
        ((n_own, width), F32),
        ((n_own, 128), F32),
        ((width, 128), F32),
        ((16, width), F32),
        ((n_own, width), BF),
    ]
    order = kept[:12] + [kept[14], kept[12], kept[13]]
    scratch = [
        ((nlane, 128), F32),
        ((hr, 128), F32),
        ((2, rows, width // 2), BF),
        ((2, rows, width // 2), BF),
        ((2, rows, half_ff // 2), BF),
        ((2, rows, half_ff // 2), BF),
        (zyc + (nlane, 256), F32),
        (zyc + (hr, 256), F32),
    ]
    scratch += weights + order
    scratch += [((n_all, width), BF), ((n_own, width), BF), ((128, 128), F32), ((8, half_ff), F32)]
    n = 15
    vm = pl.BlockSpec(memory_space=pltpu.VMEM)
    hb = pl.BlockSpec(memory_space=ANY)
    sm = pl.BlockSpec(memory_space=pltpu.SMEM)
    return pl.pallas_call(
        forward_kernel,
        out_shape=[jax.ShapeDtypeStruct(s, d) for s, d in weights + kept],
        in_specs=[sm, hb] + [vm] * 6,
        out_specs=[hb] * 19,
        scratch_shapes=[pltpu.VMEM(s, d) for s, d in scratch]
        + [
            dma(n), dma(n, 3), dma(n, 3), dma(n, 3), dma(n, 3),
            dma(3), dma(20),
        ],
        compiler_params=pltpu.CompilerParams(
            collective_id=1, has_side_effects=True, vmem_limit_bytes=60 * 2**20
        ),
        name="forward",
    )(lengths, tokens, w_qkv, w_attn, w_inner, w_outer, w_proj, vectors)


class Reduce:
    def __init__(self, me, pieces, sems):
        self.me, self.pieces = me, pieces
        self.ds, self.dr, self.ss, self.rs = sems
        self.waits, self.sent = [], []
        self.squares = jnp.zeros((1, 1), F32)

    def go(self, copy):
        copy.start()
        self.waits.append(copy)

    def arrived(self, ref, ssem, rsem):
        remote(ref, ref, ssem, rsem, self.me.dev(c=1 - self.me.c)).wait_recv()

    def region(self, p, stage, **at):
        order, src = self.pieces[p][0], self.pieces[p][2]
        me, done = self.me, order[:stage]
        half = src.shape[-1] // 2
        z = at.get("z", me.z if "z" in done else None)
        y = at.get("y", me.y if "y" in done else None)
        x = at.get("x", me.x if "x" in done else None)
        zs = slice(None) if z is None else pl.ds(0, NZ - 1) if z == "three" else pl.ds(z, 1)
        ys = slice(None) if y is None else pl.ds(y, 1)
        xs = slice(None) if x is None else cols(x, half)
        return src.at[zs, ys, me.c, :, xs]

    def send(self, p, stage):
        order, got, me = self.pieces[p][0], self.pieces[p][4 + stage], self.me
        ss, rs = self.ss, self.rs
        if order[stage] == "z":
            for k in range(1, NZ):
                tz = lax.rem(me.z + k, NZ)
                part = self.region(p, stage, z=tz)
                remote(part, got.at[pl.ds(k, 1)], ss.at[p, stage], rs.at[p, stage], me.dev(z=tz)).start()
        else:
            far = 1 - (me.y if order[stage] == "y" else me.x)
            part = self.region(p, stage, **{order[stage]: far})
            dev = me.dev(**{order[stage]: far})
            remote(part, got, ss.at[p, stage], rs.at[p, stage], dev).start()
        self.sent.append((p, stage))

    def receive(self, p, stage):
        order, got = self.pieces[p][0], self.pieces[p][4 + stage]
        if order[stage] == "z":
            got = got.at[pl.ds(1, NZ - 1)]
        self.arrived(got, self.ss.at[p, stage], self.rs.at[p, stage])

    def add(self, p, stage):
        order, _, src, _, *gots = self.pieces[p]
        got, me = gots[stage], self.me
        done = order[: stage + 1]
        half = src.shape[-1] // 2
        xs = cols(me.x, half) if "x" in done else slice(None)
        ys = [(me.y, 0)] if "y" in done else [(y, y) for y in range(NY)]
        if order[stage] == "z":
            for y, i in ys:
                total = src[me.z, y, me.c, :, xs].astype(F32)
                for k in range(1, NZ):
                    total = total + got[k, i].astype(F32)
                src[me.z, y, me.c, :, xs] = total.astype(src.dtype)
            return

        def one(z):
            for y, i in ys:
                src[z, y, me.c, :, xs] = src[z, y, me.c, :, xs] + got[0 if "z" in done else z, i]

        if "z" in done:
            one(me.z)
        else:
            each(NZ, one)

    def step1(self, p):
        src, got = self.pieces[p][2], self.pieces[p][3]
        oc = 1 - self.me.c
        remote(src.at[:, :, oc], got, self.ds.at[p], self.dr.at[p], self.me.dev(c=oc)).start()
        self.sent.append((p, None))

    def step2(self, p):
        src, got, c = self.pieces[p][2], self.pieces[p][3], self.me.c
        self.arrived(got, self.ds.at[p], self.dr.at[p])

        def one(z):
            for y in range(NY):
                src[z, y, c] = src[z, y, c] + got[z, y]

        each(NZ, one)
        self.send(p, 0)

    def step3(self, p):
        self.receive(p, 0)
        self.add(p, 0)
        self.send(p, 1)

    def step4(self, p):
        self.receive(p, 1)
        self.add(p, 1)
        self.send(p, 2)

    def step5(self, p, counted=None):
        order, dst, src, _, *gots = self.pieces[p]
        me = self.me
        self.receive(p, 2)
        total = src[me.z, me.y, me.c, :, cols(me.x, src.shape[-1] // 2)].astype(F32)
        for k in range(1, NZ) if order[2] == "z" else (0,):
            total = total + gots[2][k, 0].astype(F32)
        dst[...] = total
        total = total[:counted]
        self.squares = self.squares + jnp.sum(total * total, keepdims=True)

    def end(self):
        oc = 1 - self.me.c
        for p, stage in self.sent:
            if stage is None:
                part, sem = self.pieces[p][2].at[:, :, oc], self.ds.at[p]
            else:
                axis = self.pieces[p][0][stage]
                far = "three" if axis == "z" else 1 - (self.me.y if axis == "y" else self.me.x)
                part, sem = self.region(p, stage, **{axis: far}), self.ss.at[p, stage]
            remote(part, part, sem, sem, self.me.dev(c=oc)).wait_send()
        for copy in self.waits:
            copy.wait_send()


def got_shapes(order, r, w):
    out, done = [], ""
    for axis in order:
        done += axis
        nz = NZ if axis == "z" or "z" not in done else 1
        out.append((nz, 1 if "y" in done else NY, r, w // 2 if "x" in done else w))
    return out


orders = ("yxz", "yxz", "zyx", "zyx", "yxz", "yxz", "yzx", "yxz", "yxz", "zyx", "yxz", "yxz", "yxz", "yxz")


def all_squares(me, net, total, sq4, sq8, sems):
    qs, qr, es, er = sems
    sq4[0] = jnp.broadcast_to(total, (8, 128))
    copies = []
    for k in range(1, NZ):
        copies.append(remote(sq4.at[0], sq4.at[k], qs.at[k], qr.at[k], me.dev(z=lax.rem(me.z + k, NZ))))
    for copy in copies:
        net.go(copy)
    for copy in copies:
        copy.wait_recv()

    def at_z(z):
        out = jnp.zeros((8, 128), F32)
        for k in range(NZ):
            out = out + jnp.where(lax.rem(me.z + NZ - k, NZ) == z, sq4[k], 0.0)
        return out

    sq8[0] = at_z(0) + at_z(1) + at_z(2) + at_z(3)
    copies = []
    for k, dev in enumerate(me.eights(), 1):
        copies.append(remote(sq8.at[0], sq8.at[k], es.at[k], er.at[k], dev))
    for copy in copies:
        net.go(copy)
    for copy in copies:
        copy.wait_recv()

    def at_code(w):
        out = jnp.zeros((8, 128), F32)
        for k in range(8):
            dx, dy, dc = k & 1, (k >> 1) & 1, k >> 2
            src = (
                (me.x + dx - 2 * dx * me.x)
                + 2 * (me.y + dy - 2 * dy * me.y)
                + 4 * (me.c + dc - 2 * dc * me.c)
            )
            out = out + jnp.where(src == w, sq8[k], 0.0)
        return out

    whole = at_code(0)
    for w in range(1, 8):
        whole = whole + at_code(w)
    return whole


def fold(value):
    return jnp.sum(value.reshape(-1, 8, value.shape[-1]), axis=0)


def norm_back_rows(n_rows, get_dy, hat_ref, root_ref, gain, put, acc):
    step = 48

    def body(i):
        at = rows_at(i, step)
        dy, hat = get_dy(i, at), hat_ref[at, :]
        e = dy * gain
        root = root_ref[at, 0:1]
        m1 = jnp.mean(e, axis=-1, keepdims=True)
        m2 = jnp.mean(e * hat, axis=-1, keepdims=True)
        dz = (e - m1 - hat * m2) * root
        acc[0] = acc[0] + fold(dy * hat)
        acc[1] = acc[1] + fold(dy)
        acc[2] = acc[2] + fold(dz)
        hat_ref[at, :] = dz
        put(at, dz)

    each(n_rows // step, body)


def backward_kernel(*refs):
    doc_ids, cotangent, doc_rows = refs[:3]
    (qk_h, va_h, inner_h, outer_h, xt_h, q_h, k_h, v_h, p_h, o_h, xh1_h, r1_h, g_h, gp_h, xh2_h, r2_h, proj_h, vec_h, out_h) = refs[3:22]
    outs = refs[22:32]
    small_r, qk_r, va_r, inner_r, outer_r, dx, peer_out, peer_dx, peer_small, norm_ref = outs
    scr = list(refs[32:])

    def take(n):
        got = scr[:n]
        del scr[:n]
        return got

    (inner, outer, attn, xt, q, k, v, o, xh1, gg, xh2, r2, proj, vec, cls_in, cot, df, dft) = take(18)
    (cls_grad, acc1, acc2, ffacc, vg, early, late) = take(7)
    grads = take(4)
    bufs = take(14 * 4)
    sq4, sq8 = take(2)
    lsem, rsems, xs, xr, qsems = take(1)[0], take(4), *take(2), take(4)
    do, da, dat, h1t, r1 = cot, df, dft, dft, r2
    me = Place()
    mp = me.x
    n_all, width = dx.shape
    n_own = q.shape[0]
    half_seq = n_all - n_own
    seq = 2 * half_seq
    n_full = n_own - half_seq
    full = n_full // seq
    half_ff = inner.shape[-1]
    other = me.dev(x=1 - mp)

    for i in range(4):
        grads.append(inner.at[i // 2, :, :, :, :, pl.ds(width * (i % 2), width)])
    copies = {}

    def load(name, i, src, dst):
        cp = pltpu.make_async_copy(src, dst, lsem.at[i])
        cp.start()
        copies[name] = cp

    def need(*names):
        for name in names:
            copies[name].wait()

    load("vec", 0, vec_h, vec)
    load("proj", 1, proj_h, proj)
    for s in range(full + 1):
        load("cls%d" % s, 2 + s, out_h.at[pl.ds(s * seq, 16)], cls_in.at[s])
    load("cot0", 5, cotangent.at[pl.ds(pl.multiple_of(mp * (n_full + seq), 16), n_full)], cot.at[pl.ds(0, n_full)])
    load("cot1", 6, cotangent.at[pl.ds(pl.multiple_of(n_full + mp * half_seq, 16), half_seq)], cot.at[pl.ds(n_full, half_seq)])
    load("xh2", 7, xh2_h, xh2)
    load("r2", 8, r2_h, r2)
    load("g", 9, g_h, gg.at[pl.ds(0, 2)])
    load("outer", 10, outer_h, outer)
    load("gp", 11, gp_h, gg.at[pl.ds(2, 2)])
    load("xh1", 12, xh1_h, xh1)
    load("inner", 14, inner_h, inner)
    load("attn", 15, va_h.at[1], attn)
    load("o", 16, o_h, o)
    load("q", 17, q_h, q)
    load("k", 18, k_h, k)
    load("v", 19, v_h, v)
    load("xt", 20, xt_h, xt)

    greet(me.others() + me.eights())
    pieces = []
    hr = width // (NZ * NY * NC * NX)
    n_early = early.shape[3]
    hf = half_ff // 2
    dsts, srcs = [], []
    for i, ref in enumerate((outer_r, inner_r)):
        for h in range(2):
            for j in range(2):
                dsts.append(ref.at[h, :, pl.ds(j * (hf // 2), hf // 2)])
                srcs.append(grads[2 * i + h].at[:, :, :, :, pl.ds(j * hf, hf)])
    dsts += [va_r.at[1], va_r.at[0], qk_r.at[0], qk_r.at[1]]
    dsts += [small_r.at[pl.ds(0, n_early)], small_r.at[pl.ds(n_early, hr)]]
    srcs += grads[4:] + [early, late]
    for i in range(14):
        pieces.append((orders[i], dsts[i], srcs[i]) + tuple(bufs[4 * i : 4 * i + 4]))
    net = Reduce(me, pieces, rsems)

    def go(step, *members):
        for piece in members:
            if step == 5 and piece == 12:
                net.step5(piece, hr)
            else:
                (net.step1, net.step2, net.step3, net.step4, net.step5)[step - 1](piece)

    send_out = remote(out_h, peer_out, xs.at[0], xr.at[0], other)
    net.go(send_out)

    vg[...] = jnp.zeros_like(vg)
    early[...] = jnp.zeros_like(early)
    acc1[...] = jnp.zeros_like(acc1)
    acc2[...] = jnp.zeros_like(acc2)
    ffacc[...] = jnp.zeros_like(ffacc)
    need("vec", "proj", *["cls%d" % s for s in range(full + 1)])
    row16 = lax.broadcasted_iota(jnp.int32, (16, 1), 0)
    cls = jnp.zeros((16, width), F32)
    for s in range(full + 1):
        cls = jnp.where(row16 == s, cls_in[s].astype(F32)[0:1], cls)
    cls = cls.astype(BF)
    proj_low = proj[...].astype(BF)
    query = mm(cls, proj_low).astype(BF).astype(F32)
    row8 = lax.broadcasted_iota(jnp.int32, (8, 1), 0)
    dcq = jnp.zeros((16, 128), F32)
    row_grads = []
    cands = doc_ids.shape[1]
    seq_ids = [mp * (full + 1) + s for s in range(full)] + [full]
    for s in range(full + 1):
        docs = doc_rows[seq_ids[s]].astype(F32)
        mine = 1.0 if s < full else jnp.where(mp == 0, 1.0, 0.0)
        query_s = query[s : s + 1]
        score = jnp.sum(query_s * docs, axis=-1, keepdims=True) * retrieval_scale
        e = jnp.exp(score - jnp.max(score, axis=0, keepdims=True))
        soft = e / jnp.sum(e, axis=0, keepdims=True)
        sg = (soft - jnp.where(row8 == 0, 1.0, 0.0)) * (retrieval_scale * mine)
        dcq = jnp.where(row16 == s, jnp.sum(sg * docs, axis=0, keepdims=True), dcq)
        row_grads.append(sg * query_s)
    dcq = dcq.astype(BF)
    cls_grad[...] = mm_nt(dcq, proj_low)
    proj_grad = mm_tn(cls, dcq)
    n_dev = NZ * NY * NC * NX
    table_row = lax.broadcasted_iota(jnp.int32, (TAB_DEV * n_dev // NX, 1), 0)
    table = jnp.zeros((TAB_DEV * n_dev // NX, 128), F32)
    for s in range(full + 1):
        for i in range(cands):
            table = table + jnp.where(table_row == doc_ids[seq_ids[s], i], row_grads[s][i : i + 1], 0.0)
    tr = TAB_DEV // NX
    for d in range(n_dev):
        z, y, c, x = d // 8, d // 4 % 2, d // 2 % 2, d % 2
        l = slice(x * 128, (x + 1) * 128)
        t0 = (d // 2) * TAB_DEV + x * tr
        early[z, y, c, 0:hr, l] = proj_grad[d * hr : (d + 1) * hr]
        early[z, y, c, hr : hr + tr, l] = table[t0 : t0 + tr]
    go(1, 12)

    per = seq // 48
    row48 = lax.broadcasted_iota(jnp.int32, (48, 1), 0)

    def get_dy(i, at):
        first = (row48 == 0) & (lax.rem(i, per) == 0)
        return cot[at, :].astype(F32) + jnp.where(first, cls_grad[pl.ds(i // per, 1), :], 0.0)

    def put_df(at, dz):
        df[at, :] = dz.astype(BF)

    need("cot0", "cot1", "xh2", "r2")
    norm_back_rows(n_own, get_dy, xh2, r2, vec[10:11, :], put_df, acc2)

    def turn(src, dst, n_rows):
        def body(i):
            dst[rows_at(i, 256), 0:n_rows] = jnp.transpose(src[:, lanes(i, 256)])

        each(width // 256, body)

    load("r1", 13, r1_h, r1)
    turn(df, dft, n_own)
    go(2, 12)
    n_tile = 256
    shape5 = (NZ, NY, NC, width // (NZ * NY * NC))

    def weight_grad(left, right, dst, n, at=0):
        def body(i):
            r = mm(left(), right(lanes(i + at, n_tile)))
            dst[:, :, :, :, lanes(i + at, n_tile)] = r.astype(BF).reshape(shape5 + (n_tile,))

        each(n // n_tile, body)

    need("g")
    for h in range(2):
        for j in range(2):
            weight_grad(lambda: dft[:, 0:n_own], lambda l: gg[h, :, l], grads[h], hf, j * (hf // n_tile))
            i = 2 * h + j
            go(1, i)
            if i > 1:
                go(2, i - 2)

    need("outer", "gp")
    tile = 720
    tiles = n_own // tile

    def hidden(h):
        def body(i):
            w = flat(outer[h, :, :, :, :, lanes(i, n_tile)])
            for t in range(tiles):
                at = pl.ds(t * tile, tile)
                du = (mm(df[at, :], w) * gg[2 + h, at, lanes(i, n_tile)].astype(F32)).astype(BF)
                gg[2 + h, at, lanes(i, n_tile)] = du
                ffacc[h, :, lanes(i, n_tile)] = ffacc[h, :, lanes(i, n_tile)] + fold(du.astype(F32))

        each(half_ff // n_tile, body)

    go(2, 2)
    hidden(0)
    go(2, 3)
    go(3, 12)
    hidden(1)
    load("p0", 21, p_h.at[0], gg.at[0])
    load("p1", 22, p_h.at[1], gg.at[1])
    load("wq", 23, qk_h.at[0], outer.at[0, :, :, :, :, pl.ds(0, width)])
    load("wk", 24, qk_h.at[1], outer.at[0, :, :, :, :, pl.ds(width, width)])
    load("wv", 25, va_h.at[0], outer.at[1, :, :, :, :, pl.ds(0, width)])
    need("xh1", "r1")

    def h1_turn(i):
        l = lanes(i, 256)
        h1 = (xh1[:, l] * vec[3:4, l] + vec[4:5, l]).astype(BF)
        h1t[rows_at(i, 256), 0:n_own] = jnp.transpose(h1)

    each(width // 256, h1_turn)
    for h in range(2):
        for j in range(2):
            weight_grad(lambda: h1t[:, 0:n_own], lambda l: gg[2 + h, :, l], grads[2 + h], hf, j * (hf // n_tile))
            i = 4 + 2 * h + j
            go(1, i)
            if i > 5:
                go(2, i - 2)
            if i == 5:
                go(3, 0)
            if i == 7:
                go(3, 1)
    need("inner")

    def hidden_back(i):
        at = rows_at(i, tile)
        d = mm_nt(gg[2, at, :], flat(inner[0])) + mm_nt(gg[3, at, :], flat(inner[1]))
        xh2[at, :] = d + xh2[at, :]

    each(tiles, hidden_back)
    load("p2", 26, p_h.at[2], gg.at[2])
    go(2, 6, 7)

    norm_back_rows(n_own, lambda i, at: xh2[at, :], xh1, r1, vec[3:4, :], put_df, acc1)
    need("attn", "o")

    def mixed_back(i):
        do[:, lanes(i, n_tile)] = mm(da[...], flat(attn[:, :, :, :, lanes(i, n_tile)])).astype(BF)

    each(width // n_tile, mixed_back)
    turn(da, dat, n_own)
    weight_grad(lambda: dat[:, 0:n_own], lambda l: o[:, l], grads[4], width)
    go(1, 8)
    go(3, 4, 2)

    need("q", "k", "v", "p0", "p1", "p2")
    wide = 384
    scale = HEAD_DIM**-0.5

    def attend(q0, nq, k0, slab):
        at_q = pl.ds(pl.multiple_of(q0, 16), nq)
        at_k = pl.ds(pl.multiple_of(k0, 16), seq)
        for pair in range(2):
            l = lanes(2 * slab + pair)
            qp, kp, dop = q[at_q, l], k[at_k, l], do[at_q, l]
            pb = gg[slab, at_q, 2 * wide * pair : 2 * wide * (pair + 1)]
            p = pb.astype(F32)
            pd = p * mm_nt(dop, stack_heads(v[at_k, l], wide))
            ds, pbs = [], []
            for h in range(2):
                at = slice(h * wide, (h + 1) * wide)
                ds.append((pd[:, at] - p[:, at] * jnp.sum(pd[:, at], axis=-1, keepdims=True)).astype(BF))
                pbs.append(pb[:, h * wide : h * wide + seq])
            q[at_q, l] = (mm(jnp.concatenate(ds, axis=1), stack_heads(kp, wide)) * scale).astype(BF)
            ds = jnp.concatenate([d[:, 0:seq] for d in ds], axis=0)
            k[at_k, l] = (mm_tn(ds, stack_heads(qp)) * scale).astype(BF)
            v[at_k, l] = mm_tn(jnp.concatenate(pbs, axis=0), stack_heads(dop)).astype(BF)

    slabs = p_h.shape[0]
    jobs = (
        ([(2, 8), (4, 0, 1)], [(3, 5)], [(3, 3), (4, 12)]),
        ([(4, 4)], [(3, 6)], []),
        ([(3, 7)], [(4, 5)], [(4, 2)]),
    )

    def tokens_back(at, own):
        d = mm_nt(k[at, :], flat(outer[0, :, :, :, :, width : 2 * width]))
        d = d + mm_nt(v[at, :], flat(outer[1, :, :, :, :, 0:width]))
        if own:
            d = d + mm_nt(q[at, :], flat(outer[0, :, :, :, :, 0:width])) + xh1[at, :]
            o[at, :] = d.astype(BF)
        else:
            df[0:half_seq, :] = d.astype(BF)

    keeps = []

    def send_dx(i, src, at):
        net.go(remote(src, peer_dx.at[at], xs.at[1 + i], xr.at[1 + i], other))
        cp = pltpu.make_async_copy(src, dx.at[at], lsem.at[27 + i])
        cp.start()
        keeps.append(cp)

    need("wq", "wk", "wv")
    for s in range(full):
        with_jobs(slabs, lambda i: attend(s * seq, seq, s * seq, i), go, jobs[s])
        tokens_back(pl.ds(s * seq, seq), True)
        size = seq if s == 0 else half_seq
        send_dx(s, o.at[pl.ds(s * seq, size)], pl.ds(s * seq, size))
    with_jobs(slabs, lambda i: attend(n_full, half_seq, n_full, i), go, jobs[full])
    need("xt")
    weight_grad(lambda: xt[...], lambda l: v[:, l], grads[5], width)
    go(1, 9)
    send_dx(2, o.at[pl.ds(n_full - half_seq, half_seq)], pl.ds(n_full - half_seq, half_seq))
    weight_grad(lambda: xt[:, 0:n_own], lambda l: q[:, l], grads[6], width)
    go(1, 10)
    go(2, 9)
    go(4, 6)
    weight_grad(lambda: xt[...], lambda l: k[:, l], grads[7], width)
    go(1, 11)
    go(2, 10)
    go(3, 8)
    go(4, 3)
    tokens_back(pl.ds(n_full, half_seq), True)
    go(2, 11)
    tokens_back(pl.ds(n_own, half_seq), False)

    vg[0:1, :] = jnp.sum(q[...].astype(F32), axis=0, keepdims=True)
    vg[1:2, :] = jnp.sum(v[...].astype(F32), axis=0, keepdims=True)
    vg[2:3, :] = jnp.sum(acc1[2], axis=0, keepdims=True)
    vg[3:4, :] = jnp.sum(acc1[0], axis=0, keepdims=True)
    vg[4:5, :] = jnp.sum(acc1[1], axis=0, keepdims=True)
    for h in range(2):
        both = jnp.sum(ffacc[h], axis=0, keepdims=True)
        for x in range(NX):
            for j in range(2):
                at = j * hf + x * (hf // 2)
                vg[5 + NX * x + h : 6 + NX * x + h, j * (hf // 2) : (j + 1) * (hf // 2)] = both[:, at : at + hf // 2]
    vg[9:10, :] = jnp.sum(acc2[2], axis=0, keepdims=True)
    vg[10:11, :] = jnp.sum(acc2[0], axis=0, keepdims=True)
    vg[11:12, :] = jnp.sum(acc2[1], axis=0, keepdims=True)
    turned = jnp.transpose(vg[...])
    for d in range(n_dev):
        z, y, c, x = d // 8, d // 4 % 2, d // 2 % 2, d % 2
        late[z, y, c, :, x * 128 : (x + 1) * 128] = turned[d * hr : (d + 1) * hr]
    go(1, 13)
    go(2, 13)
    go(4, 7)
    go(5, 0, 1, 4, 5, 12)
    go(3, 10)
    go(3, 11)
    go(4, 8)
    go(3, 9)
    go(4, 10)
    go(3, 13)
    send_dx(3, o.at[pl.ds(n_full, half_seq)], pl.ds(n_full, half_seq))
    go(4, 9)
    go(4, 11)
    send_dx(4, df.at[pl.ds(0, half_seq)], pl.ds(n_own, half_seq))
    go(4, 13)
    go(5, 2, 3, 6, 7, 8, 10, 9)
    go(5, 11, 13)
    net.go(remote(small_r, peer_small, xs.at[6], xr.at[6], other))
    norm_ref[...] = all_squares(me, net, net.squares, sq4, sq8, qsems)
    parts = [pl.ds(0, seq)] + [pl.ds(seq + i * half_seq, half_seq) for i in range(4)]
    for i, ref in enumerate([peer_out] + [peer_dx.at[at] for at in parts] + [peer_small]):
        net.arrived(ref, xs.at[i], xr.at[i])
    for cp in keeps:
        cp.wait()
    net.end()


def backward_fast(doc_ids, cotangent, doc_rows, saved, rows):
    (qk, va, inner, outer, xt, q, k, v, p, o, xh1, r1, g, gp, xh2, r2, proj, vec, out_own) = saved
    n_own, width = q.shape
    n_all = k.shape[0]
    half_ff = inner.shape[-1]
    zyc = (NZ, NY, NC)
    hr = rows // NX
    n_early = hr + 8
    small_rows = n_early + hr
    ins = [doc_ids, cotangent, doc_rows] + list(saved)
    out_shape = [
        ((small_rows, 128), F32),
        ((2, rows, width // 2), F32),
        ((2, rows, width // 2), F32),
        ((2, rows, half_ff // 2), F32),
        ((2, rows, half_ff // 2), F32),
        ((n_all, width), BF),
        ((n_own, width), BF),
        ((n_all, width), BF),
        ((small_rows, 128), F32),
        ((8, 128), F32),
    ]
    like = lambda a: (a.shape, a.dtype)
    wide = width // 128 * 128
    scratch = [
        like(inner), like(outer), (va.shape[1:], BF), like(xt), like(q), like(k), like(v), like(o),
        like(xh1), ((4,) + g.shape[1:], BF), like(xh2), like(r2), like(proj), like(vec),
        ((3, 16, width), BF), ((n_own, width), BF), ((n_own, width), BF),
        ((width, wide), BF),
        ((16, width), F32), ((3, 8, width), F32), ((3, 8, width), F32), ((2, 8, half_ff), F32),
        ((128, width), F32), (zyc + (n_early, 256), F32), (zyc + (hr, 256), F32),
    ]
    sizes = [half_ff] * 4 + [width] * 4
    scratch += [(zyc + (rows, w), BF) for w in sizes[:4]]
    smalls = [(n_early, 256, F32), (hr, 256, F32)]
    for i, (r, w, dt) in enumerate([(rows, width, BF)] * 12 + smalls):
        scratch += [((NZ, NY, r, w), dt)] + [(shape, dt) for shape in got_shapes(orders[i], r, w)]
    scratch += [((NZ, 8, 128), F32), ((8, 8, 128), F32)]
    vm = pl.BlockSpec(memory_space=pltpu.VMEM)
    hb = pl.BlockSpec(memory_space=ANY)
    sm = pl.BlockSpec(memory_space=pltpu.SMEM)
    n = 14
    return pl.pallas_call(
        backward_kernel,
        out_shape=[jax.ShapeDtypeStruct(s, d) for s, d in out_shape],
        in_specs=[sm, hb, vm] + [hb] * 19,
        out_specs=[vm] * 5 + [hb, hb, hb, vm, vm],
        scratch_shapes=[pltpu.VMEM(s, d) for s, d in scratch]
        + [
            dma(32), dma(n), dma(n), dma(n, 3), dma(n, 3),
            dma(7), dma(7), dma(NZ), dma(NZ), dma(8), dma(8),
        ],
        compiler_params=pltpu.CompilerParams(
            collective_id=2, has_side_effects=True, vmem_limit_bytes=63 * 2**20
        ),
        name="backward",
    )(*ins)


def finish_kernel(*refs):
    small_r, peer_small, qk_r, va_r, inner_r, outer_r, total = refs[:7]
    out_own, peer_out, dx, peer_dx = refs[7:11]
    params = [refs[11 + 3 * i : 14 + 3 * i] for i in range(6)]
    outs = refs[29:51]
    turn, sem, lo, hi, mid = refs[51:]
    out_tokens, input_grad, norm = outs[0:3]
    news = [outs[3 + 3 * i : 6 + 3 * i] for i in range(6)]
    table_grad = outs[21]
    mp = lax.axis_index("mp")
    n_own = out_own.shape[0]
    n_all = dx.shape[0]
    half_seq = n_all - n_own
    n_full = n_own - half_seq
    seq = 2 * half_seq
    copies = []
    for i, (src, first) in enumerate(((out_own, mp), (peer_out, 1 - mp))):
        at = pl.multiple_of(first * (n_full + seq), 16)
        copies.append((src.at[pl.ds(0, n_full)], out_tokens.at[pl.ds(at, n_full)]))
        at = pl.multiple_of(n_full + first * half_seq, 16)
        copies.append((src.at[pl.ds(n_full, half_seq)], out_tokens.at[pl.ds(at, half_seq)]))
    copies = [pltpu.make_async_copy(s, d, sem.at[i]) for i, (s, d) in enumerate(copies)]
    for cp in copies:
        cp.start()
    lo[...] = dx[0:n_full].astype(F32)
    hi[...] = peer_dx[0:n_full].astype(F32)
    own_mid = dx[n_full:n_own].astype(F32) + peer_dx[n_own:n_all].astype(F32)
    peer_mid = peer_dx[n_full:n_own].astype(F32) + dx[n_own:n_all].astype(F32)
    mid[pl.ds(pl.multiple_of(mp * half_seq, 16), half_seq)] = own_mid
    mid[pl.ds(pl.multiple_of((1 - mp) * half_seq, 16), half_seq)] = peer_mid
    grads = (
        (lo, pl.multiple_of(mp * (n_full + seq), 16), n_full),
        (hi, pl.multiple_of((1 - mp) * (n_full + seq), 16), n_full),
        (mid, n_full, seq),
    )
    for i, (src, at, n) in enumerate(grads):
        cp = pltpu.make_async_copy(src, input_grad.at[pl.ds(at, n)], sem.at[4 + i])
        cp.start()
        copies.append(cp)

    root = jnp.sqrt(total[...])
    norm[0, 0] = jnp.max(root)
    clip = clip_norm / jnp.maximum(root[0:1, 0:1], clip_norm)
    hf = inner_r.shape[-1]
    hr = params[4][0].shape[0] // 2
    nvec, nlane = params[5][0].shape
    tr = table_grad.shape[0] // 2

    def adam(which, at, g, dec, rate):
        w, m, s = (ref[at] for ref in params[which])
        for ref, new in zip(news[which], adamw_update(w, m, s, g * clip, dec, rate)):
            ref[at] = new

    for j in range(3):
        g = qk_r[j] if j < 2 else va_r[0]
        adam(0, (j,), g, decay_rate, learn_rate)
    adam(1, (slice(None), slice(None)), va_r[1], decay_rate, learn_rate)
    for which, ref in ((2, inner_r), (3, outer_r)):
        for h in range(2):
            adam(which, (slice(None), slice(h * hf, (h + 1) * hf)), ref[h], decay_rate, learn_rate)
    turn[...] = jnp.zeros_like(turn)
    turn[0:nlane] = small_r[hr + 8 : hr + 8 + nlane]
    adam(5, (slice(None), slice(None)), jnp.transpose(turn[...])[0:nvec, 0:nlane], 0.0, vector_rate)
    for block, first in ((small_r, mp), (peer_small, 1 - mp)):
        at = pl.ds(pl.multiple_of(first * hr, 8), hr)
        adam(4, (at, slice(None)), block[0:hr], decay_rate, learn_rate)
    own_t, peer_t = small_r[hr : hr + tr], peer_small[hr : hr + tr]
    table_grad[0:tr] = jnp.where(mp == 0, own_t, peer_t)
    table_grad[tr : 2 * tr] = jnp.where(mp == 0, peer_t, own_t)
    for cp in copies:
        cp.wait()


def finish_fast(reduced, out_own, params, n_rows):
    (small_r, qk_r, va_r, inner_r, outer_r, dx, peer_out, peer_dx, peer_small, total) = reduced
    n_own, width = out_own.shape
    n_all = dx.shape[0]
    half_seq = n_all - n_own
    like = lambda a: jax.ShapeDtypeStruct(a.shape, a.dtype)
    vm = pl.BlockSpec(memory_space=pltpu.VMEM)
    hb = pl.BlockSpec(memory_space=ANY)
    sm = pl.BlockSpec(memory_space=pltpu.SMEM)
    out_shape = [
        jax.ShapeDtypeStruct((n_rows, width), BF),
        jax.ShapeDtypeStruct((n_rows, width), F32),
        jax.ShapeDtypeStruct((1, 1), F32),
    ]
    out_shape += [like(a) for a in params] + [jax.ShapeDtypeStruct((TAB_DEV, 128), F32)]
    n_full = n_own - half_seq
    outs = pl.pallas_call(
        finish_kernel,
        out_shape=out_shape,
        in_specs=[vm] * 29,
        out_specs=[hb, hb, sm] + [vm] * 19,
        scratch_shapes=[
            pltpu.VMEM((128, 128), F32),
            dma(7),
            pltpu.VMEM((n_full, width), F32),
            pltpu.VMEM((n_full, width), F32),
            pltpu.VMEM((2 * half_seq, width), F32),
        ],
        compiler_params=pltpu.CompilerParams(vmem_limit_bytes=63 * 2**20),
        name="finish",
    )(small_r, peer_small, qk_r, va_r, inner_r, outer_r, total, out_own, peer_out, dx, peer_dx, *params)
    return tuple(outs[:2]) + (outs[2].reshape(()),) + tuple(outs[3:])


def gather_plain(shards, small, rows):
    def both(v, axis):
        v = lax.all_gather(v, "dp", axis=axis, tiled=True)
        return lax.all_gather(v, "mp", axis=2, tiled=True)

    return [both(small[None], 0)] + [both(v, 1) for v in shards]


def reduce_plain(grads, small, own_out, own_dx, rows):
    def both(v, axis, wide):
        v = lax.psum_scatter(v.astype(F32), "mp", scatter_dimension=wide, tiled=True)
        return lax.psum_scatter(v, "dp", scatter_dimension=axis, tiled=True)

    small_sum = both(small, 0, 2)[0]
    sums = [both(g, 1, 2) for g in grads]
    ox = 1 - lax.axis_index("mp")
    swap = [(0, 1), (1, 0)]
    peer_out = lax.ppermute(own_out, "mp", swap)
    peer_dx = lax.ppermute(own_dx, "mp", swap)
    peer_small = lax.ppermute(small_sum, "mp", swap)
    squares = sum(squared(g) for g in sums) + squared(small_sum[:-4])
    total = lax.psum(squares, ("dp", "mp"))
    return [small_sum] + sums + [peer_out, peer_dx, peer_small, jnp.full((8, 128), total)]


def forward_plain(lengths, tokens, w_qkv, w_attn, w_inner, w_outer, w_proj, vectors):
    mp = lax.axis_index("mp")
    n_dp = lax.axis_size("dp")
    seqs = lengths.shape[0]
    all_rows, width = tokens.shape
    seq_len = all_rows // seqs
    full = seqs // 2
    n_full, n_half = full * seq_len, seq_len // 2
    n_own = n_full + n_half
    heads = width // HEAD_DIM
    rows, half_ff = w_qkv.shape[1], w_inner.shape[1]
    nvec, vec_lanes = vectors.shape
    half_rows = rows // 2
    score_scale = HEAD_DIM ** (-0.5)

    def two(v):
        return v.reshape(rows, 2, half_ff // 2).transpose(1, 0, 2)

    qk_s = w_qkv[:2].astype(BF)
    va_s = jnp.stack([w_qkv[2], w_attn]).astype(BF)
    vec_pad = jnp.pad(vectors, ((0, 0), (0, 128 - vec_lanes)))
    proj_half = lax.dynamic_slice_in_dim(w_proj, mp * half_rows, half_rows, 0)
    small_s = jnp.concatenate([proj_half, vec_pad], axis=0)
    small_g, qk, va, inner, outer = gather_plain(
        [qk_s, va_s, two(w_inner.astype(BF)), two(w_outer.astype(BF))], small_s, rows
    )
    small_g = small_g.reshape(n_dp, half_rows + nvec, 2, 128)
    proj = small_g[:, :half_rows].transpose(0, 2, 1, 3).reshape(width, 128)
    vec = small_g[:, half_rows:, :, :vec_lanes].transpose(1, 0, 2, 3).reshape(nvec, width)
    ff_rows = nvec - 8
    b_inner = vec[5 : 5 + ff_rows].reshape(2, 2, half_ff // 2).transpose(1, 0, 2).reshape(2, half_ff)

    a0 = mp * (n_full + seq_len)
    h0 = n_full + mp * n_half
    o0 = n_full + (1 - mp) * n_half
    x_all = jnp.concatenate(
        [
            lax.dynamic_slice_in_dim(tokens, a0, n_full, 0),
            lax.dynamic_slice_in_dim(tokens, h0, n_half, 0),
            lax.dynamic_slice_in_dim(tokens, o0, n_half, 0),
        ]
    )
    x_own = x_all[:n_own]
    my_seqs = jnp.concatenate([mp * (full + 1) + jnp.arange(full), jnp.array([full])])
    my_len = lengths[my_seqs]
    pos = jnp.arange(seq_len)
    pos_last = jnp.where(pos < n_half, pos + mp * n_half, pos - n_half + (1 - mp) * n_half)
    valids = (pos[None, :] < my_len[:full, None], pos_last[None, :] < my_len[full:, None])

    q = (jnp.dot(x_own, qk[0], preferred_element_type=F32) + vec[0]).astype(BF)
    k = jnp.dot(x_all, qk[1], preferred_element_type=F32).astype(BF)
    v = (jnp.dot(x_all, va[0], preferred_element_type=F32) + vec[1]).astype(BF)
    probs, outs = [], []
    for qh, kh, vh, valid in zip(*(halves(t, n_full, seq_len) for t in (q, k, v)), valids):
        s = jnp.einsum("gqhe,gkhe->ghqk", qh, kh, preferred_element_type=F32) * score_scale
        s = jnp.where(valid[:, None, None, :], s, -1000000000.0)
        pb = jax.nn.softmax(s, axis=-1).astype(BF)
        o = jnp.einsum("ghqk,gkhe->gqhe", pb, vh, preferred_element_type=F32)
        outs.append(o.reshape(-1, width).astype(BF))
        probs.append(pb.reshape((-1,) + pb.shape[2:]))
    mixed = jnp.concatenate(outs)

    def norm(z):
        centred = z - jnp.mean(z, axis=-1, keepdims=True)
        root = lax.rsqrt(jnp.mean(centred * centred, axis=-1, keepdims=True) + ln_epsilon)
        return centred * root, jnp.broadcast_to(root, (n_own, 128))

    attn = jnp.einsum("te,de->td", mixed, va[1], preferred_element_type=F32)
    xh1, r1 = norm(x_own.astype(F32) + attn + vec[2])
    h1 = xh1 * vec[3] + vec[4]
    u = jnp.einsum("td,hdf->htf", h1.astype(BF), inner, preferred_element_type=F32) + b_inner[:, None, :]
    tail = 0.5 * (1.0 + lax.erf(u * 0.7071067811865476))
    g = (u * tail).astype(BF)
    gp = (tail + u * (0.3989422804014327 * jnp.exp(-0.5 * u * u))).astype(BF)
    f = jnp.einsum("htf,hdf->td", g, outer, preferred_element_type=F32)
    xh2, r2 = norm(h1 + f + vec[5 + ff_rows])
    out_own = (xh2 * vec[6 + ff_rows] + vec[7 + ff_rows]).astype(BF)
    vec = jnp.pad(vec, ((0, 16 - nvec), (0, 0)))
    return [qk, va, inner, outer, x_all, q, k, v, *probs, mixed, xh1, r1, g, gp, xh2, r2, proj, vec, out_own]


def halves(t, n_full, seq_len):
    heads = t.shape[1] // HEAD_DIM
    last = t.shape[0] - n_full
    return (
        t[:n_full].reshape(n_full // seq_len, seq_len, heads, HEAD_DIM),
        t[n_full:].reshape(1, last, heads, HEAD_DIM),
    )


def pass_plain(lengths, tokens, cotangent, doc_ids, doc_rows, w_qkv, w_attn, w_inner, w_outer, w_proj, vectors):
    mp = lax.axis_index("mp")
    n_dp, n_mp = lax.axis_size("dp"), lax.axis_size("mp")
    seqs = lengths.shape[0]
    all_rows, width = tokens.shape
    seq_len = all_rows // seqs
    full = seqs // 2
    n_full, n_half = full * seq_len, seq_len // 2
    n_own = n_full + n_half
    rows, half_ff = w_qkv.shape[1], w_inner.shape[1]
    half_rows = rows // 2
    nvec, vec_lanes = vectors.shape
    ff_rows = nvec - 8
    score_scale = HEAD_DIM ** (-0.5)

    saved = forward_plain(lengths, tokens, w_qkv, w_attn, w_inner, w_outer, w_proj, vectors)
    (qk, va, inner, outer, x_all, q, k, v, p_ab, p_c, mixed, xh1, r1, act_low, slope, xh2, r2, proj, vec, out_own) = saved
    qk = qk.reshape(2, width, width)
    va = va.reshape(2, width, width)
    inner = inner.reshape(2, width, half_ff)
    outer = outer.reshape(2, width, half_ff)
    x_own = x_all[:n_own]
    proj = proj.astype(BF)
    a0 = mp * (n_full + seq_len)
    h0 = n_full + mp * n_half
    cot = jnp.concatenate(
        [lax.dynamic_slice_in_dim(cotangent, a0, n_full, 0), lax.dynamic_slice_in_dim(cotangent, h0, n_half, 0)]
    )
    my_seqs = jnp.concatenate([mp * (full + 1) + jnp.arange(full), jnp.array([full])])

    n_mine = full + 1
    mine = jnp.where((jnp.arange(n_mine) < full) | (mp == 0), 1.0, 0.0).astype(F32)
    cls_low = out_own[:: seq_len][:n_mine]
    docs = doc_rows[my_seqs].astype(F32)
    ids = doc_ids[my_seqs]
    query = jnp.dot(cls_low, proj, preferred_element_type=F32).astype(BF)
    query_float = query.astype(F32)
    doc_scores = jnp.einsum("gp,gkp->gk", query_float, docs, precision=highest_mode) * retrieval_scale
    soft = jax.nn.softmax(doc_scores, axis=-1)
    target = (jnp.arange(doc_scores.shape[1]) == 0).astype(F32)
    score_grad = (soft - target[None, :]) * retrieval_scale * mine[:, None]
    query_grad = jnp.einsum("gk,gkp->gp", score_grad, docs, precision=highest_mode).astype(BF)
    row_grads = score_grad[:, :, None] * query_float[:, None, :]
    cls_grad = jnp.einsum("gp,dp->gd", query_grad, proj, preferred_element_type=F32)
    proj_grad = jnp.einsum("gd,gp->dp", cls_low, query_grad, preferred_element_type=F32)
    table_rows = TAB_DEV * n_dp
    one_hot = (jnp.arange(table_rows)[:, None] == ids.reshape(1, -1)).astype(F32)
    table_local = jnp.dot(one_hot, row_grads.reshape(-1, row_grads.shape[2]), precision=highest_mode)

    def norm_back(dy, hat, root, gain):
        e = dy * gain
        back_ = e - jnp.mean(e, axis=-1, keepdims=True) - hat * jnp.mean(e * hat, axis=-1, keepdims=True)
        return back_ * root[:, :1], jnp.sum(dy * hat, axis=0), jnp.sum(dy, axis=0)

    dy = cot.astype(F32)
    first_rows = jnp.arange(n_mine) * seq_len
    dy = dy.at[first_rows].add(cls_grad)
    dz2, dg2, dc2 = norm_back(dy, xh2, r2, vec[6 + ff_rows])
    df = dz2.astype(BF)
    dg = jnp.einsum("td,hdf->htf", df, outer, preferred_element_type=F32)
    g_outer = jnp.einsum("td,htf->hdf", df, act_low, preferred_element_type=F32).astype(BF)
    du = (dg * slope.astype(F32)).astype(BF)
    normed_low = (xh1 * vec[3] + vec[4]).astype(BF)
    g_inner = jnp.einsum("td,htf->hdf", normed_low, du, preferred_element_type=F32).astype(BF)
    dh1 = jnp.einsum("htf,hdf->td", du, inner, preferred_element_type=F32) + dz2
    dz1, dg1, dc1 = norm_back(dh1, xh1, r1, vec[3])
    da = dz1.astype(BF)
    do = jnp.dot(da, va[1], preferred_element_type=F32).astype(BF)
    g_attn = jnp.einsum("td,te->de", da, mixed, preferred_element_type=F32)
    dqs, dks, dvs = [], [], []
    probs_of = (p_ab.reshape(full, -1, seq_len, seq_len), p_c.reshape(1, -1, n_half, seq_len))
    for qh, kh, vh, doh, pb in zip(*(halves(t, n_full, seq_len) for t in (q, k, v, do)), probs_of):
        probs = pb.astype(F32)
        dp_ = jnp.einsum("gqhe,gkhe->ghqk", doh, vh, preferred_element_type=F32)
        delta = jnp.sum(probs * dp_, axis=-1, keepdims=True)
        ds_ = (probs * (dp_ - delta)).astype(BF)
        dqs.append((jnp.einsum("ghqk,gkhe->gqhe", ds_, kh, preferred_element_type=F32) * score_scale).reshape(-1, width))
        dks.append((jnp.einsum("ghqk,gqhe->gkhe", ds_, qh, preferred_element_type=F32) * score_scale).reshape(-1, width))
        dvs.append(jnp.einsum("ghqk,gqhe->gkhe", pb, doh, preferred_element_type=F32).reshape(-1, width))
    dq = jnp.concatenate(dqs).astype(BF)
    dk = jnp.concatenate(dks).astype(BF)
    dv = jnp.concatenate(dvs).astype(BF)
    g_q = jnp.einsum("td,te->de", x_own, dq, preferred_element_type=F32)
    g_k = jnp.einsum("td,te->de", x_all, dk, preferred_element_type=F32)
    g_v = jnp.einsum("td,te->de", x_all, dv, preferred_element_type=F32)
    g_qk = jnp.stack([g_q, g_k]).astype(BF)
    g_va = jnp.stack([g_v, g_attn]).astype(BF)
    dx_own = jnp.einsum("te,de->td", dq, qk[0], preferred_element_type=F32) + dz1
    dx_all = jnp.einsum("te,de->td", dk, qk[1], preferred_element_type=F32)
    dx_all = dx_all + jnp.einsum("te,de->td", dv, va[0], preferred_element_type=F32)
    dx = jnp.concatenate([dx_all[:n_own] + dx_own, dx_all[n_own:]]).astype(BF)
    db_inner = jnp.sum(du.astype(F32), axis=1)
    db_inner = db_inner.reshape(2, 2, half_ff // 2).transpose(1, 0, 2).reshape(ff_rows, width)
    vec_grad = jnp.concatenate(
        [
            jnp.stack(
                [
                    jnp.sum(dq.astype(F32), axis=0),
                    jnp.sum(dv.astype(F32), axis=0),
                    jnp.sum(dz1, axis=0),
                    dg1,
                    dc1,
                ]
            ),
            db_inner,
            jnp.stack([jnp.sum(dz2, axis=0), dg2, dc2]),
        ]
    )
    vg = vec_grad.reshape(nvec, n_dp, 2, vec_lanes).transpose(1, 0, 2, 3)
    vg = jnp.pad(vg, ((0, 0), (0, 0), (0, 0), (0, 128 - vec_lanes))).reshape(n_dp, nvec, 256)
    pg = proj_grad.reshape(n_dp, 2, half_rows, 128).transpose(0, 2, 1, 3).reshape(n_dp, half_rows, 256)
    tg = table_local.reshape(n_dp, 2, TAB_DEV // 2, 128).transpose(0, 2, 1, 3).reshape(n_dp, TAB_DEV // 2, 256)
    small = jnp.concatenate([pg, vg, tg], axis=1)

    return out_own, dx, *reduce_plain([g_qk, g_va, g_inner, g_outer], small, out_own, dx, rows)


def local(
    tokens, cotangent, lengths, doc_ids, doc_rows,
    w_qkv, m_qkv, v_qkv, w_attn, m_attn, v_attn, w_inner, m_inner, v_inner,
    w_outer, m_outer, v_outer, w_proj, m_proj, v_proj, vectors, m_vectors, v_vectors,
):
    mp = lax.axis_index("mp")
    n_dp, n_mp = lax.axis_size("dp"), lax.axis_size("mp")
    fast = n_dp == NZ * NY * NC and n_mp == NX
    seqs = lengths.shape[0]
    all_rows, width = tokens.shape
    seq_len = all_rows // seqs
    full = seqs // 2
    n_full, n_half = full * seq_len, seq_len // 2
    n_own = n_full + n_half
    rows, half_ff = w_qkv.shape[1], w_inner.shape[1]
    half_rows = rows // 2
    nvec, vec_lanes = vectors.shape
    ff_rows = nvec - 8
    score_scale = HEAD_DIM ** (-0.5)

    if fast:
        saved = forward_fast(lengths, tokens, w_qkv, w_attn, w_inner, w_outer, w_proj, vectors)
        reduced = backward_fast(doc_ids, cotangent, doc_rows, saved, rows)
        params = (w_qkv, m_qkv, v_qkv, w_attn, m_attn, v_attn, w_inner, m_inner, v_inner)
        params += (w_outer, m_outer, v_outer, w_proj, m_proj, v_proj, vectors, m_vectors, v_vectors)
        return finish_fast(reduced, saved[-1], params, all_rows)
    if not fast:
        (out_own, dx, small_r, qk_r, va_r, inner_r, outer_r, peer_out, peer_dx, peer_small, total) = pass_plain(
            lengths, tokens, cotangent, doc_ids, doc_rows, w_qkv, w_attn, w_inner, w_outer, w_proj, vectors
        )
        vector_r = small_r[half_rows : half_rows + nvec, :vec_lanes]
        table_at = half_rows + nvec

    def whole_rows(own, peer):
        lo = jnp.where(mp == 0, own[:n_own], peer[:n_own])
        hi = jnp.where(mp == 0, peer[:n_own], own[:n_own])
        return lo, hi

    lo, hi = whole_rows(out_own, peer_out)
    out_tokens = jnp.concatenate([lo, hi[n_full:], hi[:n_full]])
    lo, hi = whole_rows(dx.astype(F32), peer_dx.astype(F32))
    tail = jnp.where(mp == 0, dx[n_own:], peer_dx[n_own:]).astype(F32)
    tail_hi = jnp.where(mp == 0, peer_dx[n_own:], dx[n_own:]).astype(F32)
    input_grad = jnp.concatenate(
        [lo[:n_full], lo[n_full:] + tail_hi, hi[n_full:] + tail, hi[:n_full]]
    )

    def both_halves(at, count):
        mine_, peer_ = small_r[at : at + count], peer_small[at : at + count]
        return jnp.concatenate(
            [jnp.where(mp == 0, mine_, peer_), jnp.where(mp == 0, peer_, mine_)]
        )

    proj_r = both_halves(0, half_rows)
    table_grad = both_halves(table_at, TAB_DEV // 2)
    qkv_r = jnp.stack([qk_r[0], qk_r[1], va_r[0]])
    attn_r = va_r[1]

    def back(v):
        return v.transpose(1, 0, 2).reshape(rows, half_ff)

    inner_r, outer_r = back(inner_r), back(outer_r)
    grad_norm = jnp.sqrt(total[0, 0])
    clip = clip_norm / jnp.maximum(grad_norm, clip_norm)
    results = [out_tokens, input_grad, grad_norm]
    for w, m, s, g, dec, rate in (
        (w_qkv, m_qkv, v_qkv, qkv_r, decay_rate, learn_rate),
        (w_attn, m_attn, v_attn, attn_r, decay_rate, learn_rate),
        (w_inner, m_inner, v_inner, inner_r, decay_rate, learn_rate),
        (w_outer, m_outer, v_outer, outer_r, decay_rate, learn_rate),
        (w_proj, m_proj, v_proj, proj_r, decay_rate, learn_rate),
        (vectors, m_vectors, v_vectors, vector_r, 0.0, vector_rate),
    ):
        results += list(adamw_update(w, m, s, g * clip, dec, rate))
    return tuple(results) + (table_grad,)


def solution(mesh):
    mat = P("dp", "mp")
    rep = P("dp", None)
    qkv = P(None, "dp", "mp")
    vec = P(None, ("dp", "mp"))
    placed = (rep, rep, P("dp"), rep, P("dp", None, None), qkv, qkv, qkv)
    placed += (mat,) * 9 + (rep,) * 3 + (vec,) * 3
    given = (rep, rep, P(), qkv, qkv, qkv) + (mat,) * 9 + (rep,) * 3 + (vec,) * 3 + (rep,)
    return jax.shard_map(local, mesh=mesh, in_specs=placed, out_specs=given, check_vma=False)
```

profile of v0, /device:TPU:0, one launch (start us, length us, event | category | flops | bytes accessed | tf_op | source)
XLA Modules:
  0.0 193.6 jit_solution(1935180597080653934)
XLA Ops:
  0.7 81.4 %forward.1 = (bf16[2,4,2,2,48,768]{5,4,3,2,1,0:T(8,128)(2,1)}, bf16[2,4,2,2,48,768]{5,4,3,2,1,0:T(8,128)(2,1)}, bf16[2,4,2,2,48,1536]{5,4,3,2,1,0:T(8,128)(2,1)}...) custom-call(s32[5]{0:T(128)} %refs_0_.2, ...), custom_call_target="tpu_custom_call" | custom-call | tf_op jit(solution)/shard_map/forward/pallas_call | solution.py:596
  82.0 103.4 %backward.1 = (f32[56,128]{1,0:T(8,128)}, f32[2,48,384]{2,1,0:T(8,128)}, f32[2,48,384]{2,1,0:T(8,128)}, f32[2,48,768]{2,1,0:T(8,128)}, f32[2,48,768]{2,1,0:T(8,1...) custom-call(s32[5,8]{1,0:T(8,128)} %refs_0_.3, ...), custom_call_target="tpu_custom_call" | custom-call | tf_op jit(solution)/shard_map/backward/pallas_call | solution.py:1219
  185.4 8.0 %finish.1 = (bf16[1440,768]{1,0:T(8,128)(2,1)}, f32[1440,768]{1,0:T(8,128)}, f32[1,1]{1,0:T(1,128)}, f32[3,48,384]{2,1,0:T(8,128)}, f32[3,48,384]{2,1,0:T(8,128)...) custom-call(f32[56,128]{1,0:T(8,128)} %get-tuple-element.92.refs_0_,, ...), custom_call_target="tpu_custom_call" | custom-call | tf_op jit(solution)/shard_map/finish/pallas_call | solution.py:1325
where the time goes:
time: 194 us
  Pallas kernels  193 us (99%)
    pallas_call x1, Pallas kernels, backward_fast(): pl.pallas_call(backward_kernel, out_shape=[jax.ShapeDtypeStruct(s, d) for...  103 us
    pallas_call x1, Pallas kernels, forward_fast(): pl.pallas_call(forward_kernel, out_shape=[jax.ShapeDtypeStruct(s, d) for...  81.4 us
    pallas_call x1, Pallas kernels, finish_fast(): pl.pallas_call(finish_kernel, out_shape=out_shape, in_specs=[vm] * 29, ou...  7.99 us

commit v1 on v0

--- a/solution.py
+++ b/solution.py
@@ -273,11 +273,11 @@
             remote(ref, ref, sem, sem, self.me.dev(c=1 - c)).wait_send()
 
 
-def norm_rows(z_ref, r_ref, n_rows, put):
+def norm_rows(z_ref, r_ref, n_rows, put, start=0):
     step = 48
 
     def body(i):
-        at = rows_at(i, step)
+        at = rows_at(i, step, start)
         z = z_ref[at, :]
         centred = z - jnp.mean(z, axis=-1, keepdims=True)
         spread = jnp.mean(centred * centred, axis=-1, keepdims=True)
@@ -528,10 +528,15 @@
     def put_y(at, hat):
         out_own[at, :] = (hat * vec[10:11, :] + vec[11:12, :]).astype(BF)
 
-    norm_rows(xh2, r2, n_own, put_y)
-    save(14, xh2)
-    save(15, r2)
-    save(18, out_own)
+    cut = n_own // 96 * 48 + 48
+    for at, n, slot in ((0, cut, 0), (cut, n_own - cut, 1)):
+        norm_rows(xh2, r2, n, put_y, at)
+        for i, ref in ((14, xh2), (15, r2), (18, out_own)):
+            part = pl.ds(at, n)
+            sem = osem.at[i] if slot == 0 else osem.at[19 + (14, 15, 18).index(i)]
+            cp = pltpu.make_async_copy(ref.at[part], outs[i].at[part], sem)
+            cp.start()
+            saves.append(cp)
     go(5, 14)
     for d in range(NZ * NY * NC * NX):
         block = proj_g[d // 8, d // 4 % 2, d // 2 % 2, :, d % 2 * 128 : (d % 2 + 1) * 128]
@@ -601,7 +606,7 @@
         scratch_shapes=[pltpu.VMEM(s, d) for s, d in scratch]
         + [
             dma(n), dma(n, 3), dma(n, 3), dma(n, 3), dma(n, 3),
-            dma(3), dma(20),
+            dma(3), dma(22),
         ],
         compiler_params=pltpu.CompilerParams(
             collective_id=1, has_side_effects=True, vmem_limit_bytes=60 * 2**20

time: 194 us -> 193 us (level)
  no operation moved by 1% of the time
where the time goes in v1:
time: 193 us
  Pallas kernels  192 us (99%)
    pallas_call x1, Pallas kernels, backward_fast(): pl.pallas_call(backward_kernel, out_shape=[jax.ShapeDtypeStruct(s, d) for...  104 us
    pallas_call x1, Pallas kernels, forward_fast(): pl.pallas_call(forward_kernel, out_shape=[jax.ShapeDtypeStruct(s, d) for...  80.7 us
    pallas_call x1, Pallas kernels, finish_fast(): pl.pallas_call(finish_kernel, out_shape=out_shape, in_specs=[vm] * 29, ou...  7.99 us

profile of v1, /device:TPU:0, one launch (start us, length us, event | category | flops | bytes accessed | tf_op | source)
XLA Modules:
  0.0 193.1 jit_solution(9041983645514471352)
XLA Ops:
  0.7 80.7 %forward.1 = (bf16[2,4,2,2,48,768]{5,4,3,2,1,0:T(8,128)(2,1)}, bf16[2,4,2,2,48,768]{5,4,3,2,1,0:T(8,128)(2,1)}, bf16[2,4,2,2,48,1536]{5,4,3,2,1,0:T(8,128)(2,1)}...) custom-call(s32[5]{0:T(128)} %refs_0_.2, ...), custom_call_target="tpu_custom_call" | custom-call | tf_op jit(solution)/shard_map/forward/pallas_call | solution.py:601
  81.4 103.5 %backward.1 = (f32[56,128]{1,0:T(8,128)}, f32[2,48,384]{2,1,0:T(8,128)}, f32[2,48,384]{2,1,0:T(8,128)}, f32[2,48,768]{2,1,0:T(8,128)}, f32[2,48,768]{2,1,0:T(8,1...) custom-call(s32[5,8]{1,0:T(8,128)} %refs_0_.3, ...), custom_call_target="tpu_custom_call" | custom-call | tf_op jit(solution)/shard_map/backward/pallas_call | solution.py:1224
  184.9 8.0 %finish.1 = (bf16[1440,768]{1,0:T(8,128)(2,1)}, f32[1440,768]{1,0:T(8,128)}, f32[1,1]{1,0:T(1,128)}, f32[3,48,384]{2,1,0:T(8,128)}, f32[3,48,384]{2,1,0:T(8,128)...) custom-call(f32[56,128]{1,0:T(8,128)} %get-tuple-element.92.refs_0_,, ...), custom_call_target="tpu_custom_call" | custom-call | tf_op jit(solution)/shard_map/finish/pallas_call | solution.py:1330
